TPU v7x, 32 devices: a whole 2x2x4 slice. The times are simulated.
32 devices in a mesh: res: 8 (over z, y), dp: 4 (over x, core).
Axes of the slice: x: 2, y: 2, z: 4, core: 2. Of those that a mesh axis runs over, the one named last changes fastest.
Arguments:
- aligned_chain_features: bfloat16 [512, 256, 256], P('dp', 'res'), parts along dimension 0, may hold values from -6 to 6
- pair_representation_state: bfloat16 [1024, 256, 128], P(('dp', 'res')), parts along dimension 0, may hold values from -6 to 6
- gap_block_flags: int32 [512, 2], P('dp'), parts along dimension 0, may hold values from 0 to 1, as said below
- pair_norm_gain: float32 [128], replicated, may hold values from 0.1 to 1.9
- pair_head_weight: bfloat16 [128, 8], replicated, may hold values from -0.5 to 0.5
- horizontal_scaling_factor: float32 [256], replicated, may hold values from 0.1 to 1.9
- row_input_weight: bfloat16 [256, 1024], replicated, may hold values from -2 to 2
- horizontal_final_matrix: bfloat16 [256, 256], replicated, may hold values from -0.375 to 0.375
- vertical_scaling_factor: float32 [256], replicated, may hold values from 0.1 to 1.9
- column_input_weight: bfloat16 [256, 1024], replicated, may hold values from -2 to 2
- vertical_final_matrix: bfloat16 [256, 256], replicated, may hold values from -0.375 to 0.375
- feedforward_scaling_factor: float32 [256], replicated, may hold values from 0.1 to 1.9
- feedforward_widen_matrix: bfloat16 [256, 1024], replicated, may hold values from -0.375 to 0.375
- feedforward_shrink_matrix: bfloat16 [1024, 256], replicated, may hold values from -0.1875 to 0.1875
Outputs:
- msa_out: bfloat16 [512, 256, 256], P('dp', 'res'), parts along dimension 0
There are 4 independent parts, one for each index of `dp`. A program takes and returns all parts, laid end to end along the dimension named above; an argument that names none is the same for every part. Nothing has to cross between parts.
Inputs may be any that keep to these rules, and one draw needn't show every extreme that they name: `gap_block_flags`: row 0 holds no gap block, and every row has at least one block that is not a gap.
All inputs are finite; a program needn't handle non-finite values.
Results may differ from a plain program's by a relative error of at most 0.015.
The roundings to bfloat16 on the way count: a program that leaves them out, or rounds other values in their place, can miss the bound.
Values may be sent and summed in bfloat16 or wider, within the bound.
No kernel may reach another device: no remote copies, remote signals or barrier semaphores. Data moves between devices by JAX's collectives and lax.ppermute only.
A program may use at most 128 MiB of HBM per device.

v0:
```python
import jax
import jax.numpy as jnp
from jax import lax
from jax.sharding import PartitionSpec as P

BLOCK = 128


EPSILON = 1e-05
MASKED_SCORE = -1000000000.0


def layer_normalize(inputs, scale_gain):
    values_f = inputs.astype(jnp.float32)
    centred = values_f - jnp.mean(values_f, axis=-1, keepdims=True)
    spread = jnp.mean(centred * centred, axis=-1, keepdims=True)
    return centred * lax.rsqrt(spread + EPSILON) * scale_gain


def project(normed_bf, weights_in, head_count, head_depth):
    projected = jnp.dot(normed_bf, weights_in, preferred_element_type=jnp.float32)
    projected = projected.reshape(projected.shape[:-1] + (4, head_count, head_depth))
    queries = (projected[..., 0, :, :] * head_depth ** (-0.5)).astype(jnp.bfloat16)
    keys_bf = projected[..., 1, :, :].astype(jnp.bfloat16)
    values_bf = projected[..., 2, :, :].astype(jnp.bfloat16)
    gates = jax.nn.sigmoid(projected[..., 3, :, :])
    return (queries, keys_bf, values_bf, gates)


def attend_dense(queries, keys_bf, values_bf, bias_piece, masked):
    scores = jnp.einsum("qhd,khd->hqk", queries, keys_bf, preferred_element_type=jnp.float32)
    scores = scores + bias_piece.astype(jnp.float32)
    scores = jnp.where(masked[None, None, :], MASKED_SCORE, scores)
    weights_bf = jax.nn.softmax(scores, axis=-1).astype(jnp.bfloat16)
    return jnp.einsum("hqk,khd->qhd", weights_bf, values_bf, preferred_element_type=jnp.float32)


def body(
    aligned_chain_features,
    pair_representation_state,
    gap_block_flags,
    pair_norm_gain,
    pair_head_weight,
    horizontal_scaling_factor,
    row_input_weight,
    horizontal_final_matrix,
    vertical_scaling_factor,
    column_input_weight,
    vertical_final_matrix,
    feedforward_scaling_factor,
    feedforward_widen_matrix,
    feedforward_shrink_matrix,
):
    head_count = pair_head_weight.shape[1]
    head_depth = horizontal_final_matrix.shape[0] // head_count
    pair_normed = layer_normalize(pair_representation_state, pair_norm_gain).astype(jnp.bfloat16)
    bias_local = jnp.einsum(
        "ijc,ch->hij", pair_normed, pair_head_weight, preferred_element_type=jnp.float32
    ).astype(jnp.bfloat16)
    sequence_rows = lax.all_to_all(
        aligned_chain_features, "res", split_axis=0, concat_axis=1, tiled=True
    )
    local_seqs, residues = (sequence_rows.shape[0], sequence_rows.shape[1])
    gap_local = lax.dynamic_slice_in_dim(
        gap_block_flags, lax.axis_index("res") * local_seqs, local_seqs, 0
    )
    row_normed = layer_normalize(sequence_rows, horizontal_scaling_factor).astype(jnp.bfloat16)
    queries, keys_all, values_all, gates_all = project(
        row_normed, row_input_weight, head_count, head_depth
    )
    bias_all = lax.all_gather(bias_local, "res", axis=1, tiled=True)
    row_count = bias_all.shape[1]

    def per_sequence(sequence_entries):
        (
            sequence_queries,
            sequence_keys,
            sequence_values,
            sequence_gates,
            sequence_alignment,
            sequence_gap_row,
        ) = sequence_entries
        attended = attend_dense(
            sequence_queries,
            sequence_keys,
            sequence_values,
            bias_all,
            jnp.repeat(sequence_gap_row, BLOCK) == 1,
        )
        gated_out = (
            (attended * sequence_gates)
            .astype(jnp.bfloat16)
            .reshape(row_count, head_count * head_depth)
        )
        layer_update = jnp.dot(
            gated_out, horizontal_final_matrix, preferred_element_type=jnp.float32
        )
        return (sequence_alignment.astype(jnp.float32) + layer_update).astype(jnp.bfloat16)

    blocks_out = lax.map(
        per_sequence, (queries, keys_all, values_all, gates_all, sequence_rows, gap_local)
    )
    res_rows = lax.all_to_all(blocks_out, "res", split_axis=1, concat_axis=0, tiled=True)
    col_normed = layer_normalize(res_rows, vertical_scaling_factor).astype(jnp.bfloat16)
    col_q, col_k, col_v, col_gates = project(
        col_normed, column_input_weight, head_count, head_depth
    )
    total_seqs, local_res = (res_rows.shape[0], res_rows.shape[1])
    block_total = gap_block_flags.shape[1]
    global_res = lax.axis_index("res") * local_res + jnp.arange(local_res, dtype=jnp.int32)
    one_hot = (
        global_res[:, None] // BLOCK == jnp.arange(block_total, dtype=jnp.int32)[None, :]
    ).astype(jnp.int32)
    col_gaps = jnp.sum(gap_block_flags[:, None, :] * one_hot[None, :, :], axis=2)
    col_scores = jnp.einsum("srhd,trhd->rhst", col_q, col_k, preferred_element_type=jnp.float32)
    col_scores = jnp.where(
        (jnp.transpose(col_gaps) == 1)[:, None, None, :], MASKED_SCORE, col_scores
    )
    col_weights = jax.nn.softmax(col_scores, axis=-1).astype(jnp.bfloat16)
    col_attended = jnp.einsum(
        "rhst,trhd->srhd", col_weights, col_v, preferred_element_type=jnp.float32
    )
    col_gated = (
        (col_attended * col_gates)
        .astype(jnp.bfloat16)
        .reshape(total_seqs, local_res, head_count * head_depth)
    )
    alignment_second = (
        res_rows.astype(jnp.float32)
        + jnp.dot(col_gated, vertical_final_matrix, preferred_element_type=jnp.float32)
    ).astype(jnp.bfloat16)
    transition_normed = layer_normalize(alignment_second, feedforward_scaling_factor).astype(
        jnp.bfloat16
    )
    tr_hidden = jax.nn.relu(
        jnp.dot(transition_normed, feedforward_widen_matrix, preferred_element_type=jnp.float32)
    ).astype(jnp.bfloat16)
    return (
        alignment_second.astype(jnp.float32)
        + jnp.dot(tr_hidden, feedforward_shrink_matrix, preferred_element_type=jnp.float32)
    ).astype(jnp.bfloat16)


def solution(mesh):
    placed = (
        P("dp", "res", None),
        P(("dp", "res"), None, None),
        P("dp", None),
        P(),
        P(),
        P(),
        P(),
        P(),
        P(),
        P(),
        P(),
        P(),
        P(),
        P(),
    )
    return jax.shard_map(
        body, mesh=mesh, in_specs=placed, out_specs=P("dp", "res", None), check_vma=False
    )
```

profile of v0, /device:TPU:0, one launch (start us, length us, event | category | flops | bytes accessed | tf_op | source)
XLA Modules:
  0.0 323.5 jit_solution(15112912981060550380)
XLA Ops:
  6.5 7.4 %all-to-all-start = ((bf16[128,32,256]{2,1,0:T(8,128)(2,1)}), bf16[128,32,256]{2,1,0:T(8,128)(2,1)S(1)}, u32[]{:S(2)}, u32[]{:S(2)}) async-start(bf16[128,32,256]{2,1,0:T(8,128)(2,1)} %param.16), calls=%async_computation | async-start | bytes 4194304 | tf_op jit(solution)/shard_map/all_to_all | solution.py:60
  16.4 3.6 %fusion.55 = f32[32,256]{1,0:T(8,128)S(1)} fusion(bf16[32,256,128]{2,1,0:T(8,128)(2,1)} %param.17, f32[32,256]{1,0:T(8,128)S(1)} %broadcast_multiply_fusion.2), kind=kLoop, calls=%fused_computation.52 | loop fusion | flops 4186112 | bytes 2162688 | tf_op jit(solution)/shard_map/reduce_sum | solution.py:16
  20.0 3.5 %fusion.96 = bf16[8,32,256]{2,0,1:T(8,128)(2,1)} fusion(bf16[32,256,128]{2,1,0:T(8,128)(2,1)S(1)} %copy-done.3, f32[128]{0:T(128)S(1)} %copy-done.13, f32[32,256]{1,0:T(8,128)S(1)} %add_rsqrt_fusion.2, f32[32,256]{1,0:T(8,128)S(1)} %broadcast_multiply_fusion.2, bf16[128,8]{0,1:T(8,128)(2,1)S(1)} %copy-done.11), kind=kOutput, calls=%fused_computation.95 | convolution fusion | flops 22085632 | bytes 2296320 | tf_op jit(solution)/shard_map/ijc,ch->hij/dot_general | solution.py:57
  25.1 54.4 %all-gather.2.cloned.1.call-done = bf16[8,256,256]{2,0,1:T(8,128)(2,1)} async-done(((bf16[8,32,256]{2,0,1:T(8,128)(2,1)}), bf16[8,256,256]{2,0,1:T(8,128)(2,1)}) %all-gather.2.cloned.1.call-update) | async-done | bytes 1048592 | tf_op jit(solution)/shard_map/all_gather | solution.py:71
  87.8 4.0 %fusion.112 = (bf16[16,256,4,8,32]{1,4,3,2,0:T(8,128)(2,1)S(1)}, f32[16,256,4,8,32]{1,4,3,2,0:T(8,128)S(1)}) fusion(bf16[16,256,256,1,1]{2,1,4,3,0:T(8,128)(2,1)} %bitcast.180, bf16[4,8,32,256,1]{3,2,1,0,4:T(8,128)(2,1)S(1)} %bitcast.184), kind=kOutput, calls=%fused_computation.120 | convolution fusion | flops 2151677952 | bytes 27787264 | tf_op jit(solution)/shard_map/dot_general | solution.py:21
  91.8 3.8 %fusion.71 = (f32[16,256,8,32]{1,3,2,0:T(8,128)}, bf16[16,256,8,32]{1,3,2,0:T(8,128)(2,1)}) fusion(f32[16,256,4,8,32]{1,4,3,2,0:T(8,128)S(1)} %get-tuple-element.123), kind=kLoop, calls=%fused_computation.71 | loop fusion | flops 5242880 | bytes 14680064 | tf_op jit(solution)/shard_map/div | solution.py:26
  95.5 2.7 slice_bitcast_fusion.4
  98.3 96.3 %while.10 = (s32[]{:T(128)}, bf16[16,256,256]{2,1,0:T(8,128)(2,1)S(1)}, bf16[16,256,256]{2,1,0:T(8,128)(2,1)}, bf16[16,256,8,32]{1,3,2,0:T(8,128)(2,1)}, s32[16,...) while((s32[]{:T(128)}, ...), condition=%wide.region_7.8_spmd, body=%wide.region_4.7_spmd.sunk | while | flops 140315136 | bytes 3690369 | solution.py:100
  100.6 2.5 fusion.141
  106.7 2.5 fusion.141
  112.7 2.5 fusion.141
  118.7 2.5 fusion.141
  124.7 2.5 fusion.141
  130.8 2.5 fusion.141
  136.8 2.5 fusion.141
  142.8 2.5 fusion.141
  148.8 2.5 fusion.141
  154.8 2.5 fusion.141
  160.9 2.5 fusion.141
  166.9 2.5 fusion.141
  172.9 2.5 fusion.141
  178.9 2.5 fusion.141
  197.1 3.8 %all-to-all-start.1 = ((bf16[16,256,256]{2,0,1:T(8,128)(2,1)}), bf16[16,256,256]{2,0,1:T(8,128)(2,1)S(1)}, u32[]{:S(2)}, u32[]{:S(2)}) async-start(bf16[16,256,256]{2,0,1:T(8,128)(2,1)} %copy.54), calls=%async_computation.1 | async-start | bytes 4194304 | tf_op jit(solution)/shard_map/all_to_all | solution.py:103
  202.3 46.1 %all-to-all-done.1 = bf16[16,256,256]{2,0,1:T(8,128)(2,1)S(1)} async-done(((bf16[16,256,256]{2,0,1:T(8,128)(2,1)}), bf16[16,256,256]{2,0,1:T(8,128)(2,1)S(1)}, u32[]{:S(2)}, u32[]{:S(2)}) %all-to-all-start.1) | async-done | bytes 2097184 | tf_op jit(solution)/shard_map/all_to_all | solution.py:103
  251.0 2.5 copy.55
  254.9 4.7 %fusion.113 = (bf16[128,32,4,8,32]{0,4,3,2,1:T(8,128)(2,1)}, f32[128,32,4,8,32]{0,4,3,2,1:T(8,128)S(1)}) fusion(bf16[128,32,256,1,1]{2,0,4,3,1:T(8,128)(2,1)S(1)} %bitcast.181, bf16[4,8,32,256,1]{3,2,1,0,4:T(8,128)(2,1)S(1)} %bitcast.185), kind=kOutput, calls=%fused_computation.121 | convolution fusion | flops 2151677952 | bytes 27787264 | tf_op jit(solution)/shard_map/dot_general | solution.py:21
  259.7 5.7 %copy-done.1 = f32[128,32,4,8,32]{0,4,3,2,1:T(8,128)} copy-done((f32[128,32,4,8,32]{0,4,3,2,1:T(8,128)}, f32[128,32,4,8,32]{0,4,3,2,1:T(8,128)S(1)}, u32[]{:S(2)}) %copy-start.1) | copy-done | bytes 16777240
  265.4 9.7 %fusion.78 = f32[32,8,128,128]{2,3,1,0:T(8,128)} fusion(f32[128,32,4,8,32]{0,4,3,2,1:T(8,128)S(1)} %get-tuple-element.125, bf16[128,32,4,8,32]{0,4,3,2,1:T(8,128)(2,1)} %get-tuple-element.124), kind=kOutput, calls=%fused_computation.84 | convolution fusion | flops 270532608 | bytes 23068672 | tf_op jit(solution)/shard_map/srhd,trhd->rhst/dot_general | solution.py:115
  275.1 18.1 %fusion.114 = (f32[32,8,128]{2,1,0:T(8,128)S(1)}, f32[32,8,128,128]{2,3,1,0:T(8,128)}) fusion(f32[32,8,128,128]{2,3,1,0:T(8,128)} %fusion.78, pred[32,128]{1,0:T(8,128)(4,1)S(1)} %compare_bitcast_fusion.1), kind=kOutput, calls=%fused_computation.122 | output fusion | flops 16777344 | bytes 33689600 | tf_op jit(solution)/shard_map/sub | solution.py:119
  293.2 10.1 %fusion.74 = bf16[128,32,8,32]{0,3,2,1:T(8,128)(2,1)S(1)} fusion(f32[128,32,4,8,32]{0,4,3,2,1:T(8,128)} %copy-done.1, f32[32,8,128,128]{2,3,1,0:T(8,128)} %get-tuple-element.127, f32[32,8,128]{2,1,0:T(8,128)S(1)} %get-tuple-element.126, bf16[128,32,4,8,32]{0,4,3,2,1:T(8,128)(2,1)} %get-tuple-element.124), kind=kOutput, calls=%fused_computation.80 | convolution fusion | flops 282066944 | bytes 25296896 | tf_op jit(solution)/shard_map/rhst,trhd->srhd/dot_general | solution.py:120
  306.5 6.0 %fusion.61 = bf16[128,32,256]{2,0,1:T(8,128)(2,1)} fusion(bf16[128,32,256]{2,0,1:T(8,128)(2,1)S(1)} %get-tuple-element.129, f32[256]{0:T(256)S(1)} %copy-done.12, f32[128,32]{0,1:T(8,128)S(1)} %add_rsqrt_fusion.3, f32[128,32]{0,1:T(8,128)S(1)} %broadcast_multiply_fusion.3, bf16[1024,256]{1,0:T(8,128)(2,1)S(1)} %copy-done, bf16[256,1024]{1,0:T(8,128)(2,1)S(1)} %copy-done.10), kind=kOutput, calls=%fused_computation.58 | convolution fusion | flops 4311744512 | bytes 5276672 | tf_op jit(solution)/shard_map/dot_general | solution.py:140
  312.6 4.1 %copy.59 = bf16[128,32,256]{2,1,0:T(8,128)(2,1)} copy(bf16[128,32,256]{2,0,1:T(8,128)(2,1)} %fusion.61) | data formatting | bytes 4194304 | tf_op jit(solution)/shard_map/convert_element_type | solution.py:141
  (126 shorter events, 83.7 us)
Async XLA Ops:
  6.5 300.0 %copy-start = (bf16[1024,256]{1,0:T(8,128)(2,1)S(1)}, bf16[1024,256]{1,0:T(8,128)(2,1)}, u32[]{:S(2)}) copy-start(bf16[1024,256]{1,0:T(8,128)(2,1)} %param.29) | copy-start | bytes 1572868
  6.5 13.5 %copy-start.13 = (f32[128]{0:T(128)S(1)}, f32[128]{0:T(128)}, u32[]{:S(2)}) copy-start(f32[128]{0:T(128)} %param.19) | copy-start | bytes 1540
  6.5 13.5 %copy-start.11 = (bf16[128,8]{0,1:T(8,128)(2,1)S(1)}, bf16[128,8]{0,1:T(8,128)(2,1)}, u32[]{:S(2)}) copy-start(bf16[128,8]{0,1:T(8,128)(2,1)} %param.20) | copy-start | bytes 6148
  6.5 75.4 %all-to-all-start = ((bf16[128,32,256]{2,1,0:T(8,128)(2,1)}), bf16[128,32,256]{2,1,0:T(8,128)(2,1)S(1)}, u32[]{:S(2)}, u32[]{:S(2)}) async-start(bf16[128,32,256]{2,1,0:T(8,128)(2,1)} %param.16), calls=%async_computation | async-start | bytes 4194304 | tf_op jit(solution)/shard_map/all_to_all | solution.py:60
  14.0 65.5 %all-gather.2.cloned.1.call-start = ((), (), s32[]{:S(2)}) async-start(), calls=%async_computation.2 | async-start | bytes 1179648 | tf_op jit(solution)/shard_map/all_gather | solution.py:71
  14.0 6.0 %copy-start.3 = (bf16[32,256,128]{2,1,0:T(8,128)(2,1)S(1)}, bf16[32,256,128]{2,1,0:T(8,128)(2,1)}, u32[]{:S(2)}) copy-start(bf16[32,256,128]{2,1,0:T(8,128)(2,1)} %param.17) | copy-start | bytes 6291460
  16.4 8.5 %copy-start.7 = (s32[128,2]{0,1:T(2,128)S(1)}, s32[128,2]{0,1:T(2,128)}, u32[]{:S(2)}) copy-start(s32[128,2]{0,1:T(2,128)} %param.18) | copy-start | bytes 3076
  81.9 3.5 %copy-start.8 = (f32[256]{0:T(256)S(1)}, f32[256]{0:T(256)}, u32[]{:S(2)}) copy-start(f32[256]{0:T(256)} %param.21) | copy-start | bytes 3076
  95.5 2.8 copy-start.4
  95.5 2.8 copy-start.5
  197.1 51.2 %all-to-all-start.1 = ((bf16[16,256,256]{2,0,1:T(8,128)(2,1)}), bf16[16,256,256]{2,0,1:T(8,128)(2,1)S(1)}, u32[]{:S(2)}, u32[]{:S(2)}) async-start(bf16[16,256,256]{2,0,1:T(8,128)(2,1)} %copy.54), calls=%async_computation.1 | async-start | bytes 4194304 | tf_op jit(solution)/shard_map/all_to_all | solution.py:103
  251.0 2.6 copy-start.9
  259.7 5.7 %copy-start.1 = (f32[128,32,4,8,32]{0,4,3,2,1:T(8,128)}, f32[128,32,4,8,32]{0,4,3,2,1:T(8,128)S(1)}, u32[]{:S(2)}) copy-start(f32[128,32,4,8,32]{0,4,3,2,1:T(8,128)S(1)} %get-tuple-element.125) | copy-start | bytes 50331652
  293.2 10.1 %copy-start.2 = (f32[16,8,32,256]{3,0,1,2:T(8,128)S(1)}, f32[16,8,32,256]{3,0,1,2:T(8,128)}, u32[]{:S(2)}) copy-start(f32[16,8,32,256]{3,0,1,2:T(8,128)} %copy.55) | copy-start | bytes 12582916
  293.2 10.1 %copy-start.6 = (bf16[256,256]{1,0:T(8,128)(2,1)S(1)}, bf16[256,256]{1,0:T(8,128)(2,1)}, u32[]{:S(2)}) copy-start(bf16[256,256]{1,0:T(8,128)(2,1)} %param.26) | copy-start | bytes 393220
  303.3 3.2 copy-start.10
  303.3 3.2 copy-start.12
Sparse Core Ops, SparseCore 0:
  23.7 55.6 all-gather.1
where the time goes:
time: 325 us; the launch traced here: 323 us
  matrix products  134 us (41%)
  waiting for transfers between devices  100 us (31%)
  other arithmetic  37.7 us (12%)
  local copies, waits for them, and re-layouts  25.5 us (8%)
  between operations  13.7 us (4%)
  starting transfers between devices  11.2 us (3%)
    all_gather x1, waiting for transfers between devices, body(): bias_all = lax.all_gather(bias_local, 'res', axis=1, tiled=True)  54.4 us
    all_to_all x1, waiting for transfers between devices, body(): lax.all_to_all(blocks_out, 'res', split_axis=1, concat_axis=0, tiled=True)  46.1 us
    dot_general x16, matrix products, attend_dense(): jnp.einsum('hqk,khd->qhd', weights_bf, values_bf, preferred_element_type=...  40.3 us
    sub x16, matrix products, attend_dense(): weights_bf = jax.nn.softmax(scores, axis=-1).astype(jnp.bfloat16)  36 us
    sub x1, other arithmetic, body(): col_weights = jax.nn.softmax(col_scores, axis=-1).astype(jnp.bfloat16)  18.1 us
    dot_general x16, matrix products, per_sequence(): jnp.dot(gated_out, horizontal_final_matrix, preferred_element_type=jnp.fl...  18.1 us
    dot_general x1, matrix products, body(): jnp.einsum('rhst,trhd->srhd', col_weights, col_v, preferred_element_type=...  10.1 us
    dot_general x1, matrix products, body(): jnp.einsum('srhd,trhd->rhst', col_q, col_k, preferred_element_type=jnp.fl...  9.7 us
  transfers between devices with their start and end apart: 3, of which 2 were waited for; matrix products, arithmetic and copies ran while one was open for 5% of the time, Pallas kernels for 0%

commit v1 on v0

v1 whole, which is shorter than its diff:
```python
import functools

import jax
import jax.numpy as jnp
from jax import lax
from jax.experimental import pallas as pl
from jax.experimental.pallas import tpu as pltpu
from jax.sharding import PartitionSpec as P

BLOCK = 128
EPSILON = 1e-05
MASKED_SCORE = -1000000000.0
LANES = 128
SLAB = 16
F32 = jnp.float32
BF16 = jnp.bfloat16
VMEM_BYTES = 48 * 1024 * 1024


def layer_normalize(values_f, scale_gain):
    centred = values_f - jnp.mean(values_f, axis=-1, keepdims=True)
    spread = jnp.mean(centred * centred, axis=-1, keepdims=True)
    return centred * lax.rsqrt(spread + EPSILON) * scale_gain


def mm(lhs, rhs):
    return jnp.dot(lhs, rhs, preferred_element_type=F32)


def mm_nt(lhs, rhs):
    return lax.dot_general(lhs, rhs, (((1,), (1,)), ((), ())), preferred_element_type=F32)


def swap_matrix(outer, inner):
    size = outer * inner
    to = lax.broadcasted_iota(jnp.int32, (size, size), 0)
    come = lax.broadcasted_iota(jnp.int32, (size, size), 1)
    source = lax.rem(to, outer) * inner + lax.div(to, outer)
    return jnp.where(come == source, 1.0, 0.0).astype(BF16)


def head_lanes(rows, width, head_depth, head):
    lane = lax.broadcasted_iota(jnp.int32, (rows, width), 1)
    return (lane >= head * head_depth) & (lane < (head + 1) * head_depth)


def bias_kernel(pair_ref, gain_ref, weight_ref, out_ref, rows_scr):
    heads, local_res, residues = out_ref.shape
    channels = pair_ref.shape[2]
    step = min(4, local_res)

    def body(i, carry):
        block = pair_ref[pl.ds(i * step, step)].reshape(step * residues, channels)
        normed = layer_normalize(block.astype(F32), gain_ref[...]).astype(BF16)
        projected = mm_nt(weight_ref[...], normed)
        for j in range(step):
            rows_scr[i * step + j] = projected[:, j * residues : (j + 1) * residues]
        return carry

    lax.fori_loop(0, local_res // step, body, 0)
    rows = rows_scr[...].reshape(local_res * heads, residues).astype(BF16)
    turned = mm(swap_matrix(local_res, heads), rows)
    out_ref[...] = turned.reshape(heads, local_res, residues).astype(BF16)


def row_kernel(gap_ref, x_ref, bias_ref, gain_ref, win_ref, wout_ref, out_ref, bias_scr, p_scr, v_scr):
    groups, seqs, local_res, channels = x_ref.shape
    heads = bias_ref.shape[1]
    residues = groups * local_res
    depth = channels // heads
    per = LANES // depth
    scale = depth ** (-0.5)

    for h in range(heads):
        bias_scr[h] = bias_ref[:, h].reshape(residues, residues).astype(F32)

    def body(s, carry):
        x = x_ref[:, pl.ds(s, 1)].reshape(residues, channels)
        normed = layer_normalize(x.astype(F32), gain_ref[...]).astype(BF16)
        proj = mm(normed, win_ref[...])
        q = (proj[:, :channels] * scale).astype(BF16)
        k = proj[:, channels : 2 * channels].astype(BF16)
        v = proj[:, 2 * channels : 3 * channels].astype(BF16)
        gates = jax.nn.sigmoid(proj[:, 3 * channels :])
        key = lax.broadcasted_iota(jnp.int32, (1, residues), 1)
        gap = jnp.zeros((1, residues), jnp.int32)
        for b in range(residues // BLOCK):
            gap = jnp.where(key // BLOCK == b, gap_ref[s, b], gap)
        masked = gap == 1
        attended = []
        for g in range(heads // per):
            lanes = slice(g * LANES, (g + 1) * LANES)
            for j in range(per):
                h = g * per + j
                mine = head_lanes(residues, LANES, depth, j)
                qm = jnp.where(mine, q[:, lanes], jnp.zeros((), BF16))
                scores = mm_nt(qm, k[:, lanes]) + bias_scr[h]
                scores = jnp.where(masked, MASKED_SCORE, scores)
                e = jnp.exp(scores - jnp.max(scores, axis=-1, keepdims=True))
                w = e * (1.0 / jnp.sum(e, axis=-1, keepdims=True))
                p_scr[:, j * residues : (j + 1) * residues] = w.astype(BF16)
                v_scr[j * residues : (j + 1) * residues] = jnp.where(mine, v[:, lanes], jnp.zeros((), BF16))
            attended.append(mm(p_scr[...], v_scr[...]))
        gated = (jnp.concatenate(attended, axis=1) * gates).astype(BF16)
        result = x.astype(F32) + mm(gated, wout_ref[...])
        out_ref[:, pl.ds(s, 1)] = result.astype(BF16).reshape(groups, 1, local_res, channels)
        return carry

    lax.fori_loop(0, seqs, body, 0)


def column_kernel(
    heads, turn, gap_ref, x_ref, gain_ref, win_ref, wout_ref, gain2_ref, widen_ref, shrink_ref,
    out_ref, turned_scr, proj_scr, gated_scr, p_scr, done_scr,
):
    seqs, channels = x_ref.shape[-2 if not turn else 0], x_ref.shape[2]
    local_res = x_ref.shape[1 if turn else 0]
    depth = channels // heads
    per = LANES // depth
    halves = heads // per
    scale = depth ** (-0.5)
    batch = proj_scr.shape[0]
    slabs = local_res // SLAB if turn else 0
    swap = swap_matrix(SLAB, SLAB)
    if not turn:
        turned_scr[...] = x_ref[...]
    for c in range(slabs):
        for g in range(seqs // SLAB):
            block = x_ref[g * SLAB : (g + 1) * SLAB, c * SLAB : (c + 1) * SLAB]
            turned = mm(swap, block.reshape(SLAB * SLAB, channels))
            turned_scr[c * SLAB : (c + 1) * SLAB, g * SLAB : (g + 1) * SLAB] = turned.astype(
                BF16
            ).reshape(SLAB, SLAB, channels)

    masked = gap_ref[...] == 1

    def body(i, carry):
        x = turned_scr[pl.ds(i * batch, batch)].reshape(batch * seqs, channels)
        normed = layer_normalize(x.astype(F32), gain_ref[...]).astype(BF16)
        proj_scr[...] = mm(normed, win_ref[...]).reshape(batch, seqs, 4 * channels)
        for r in range(batch):
            q = (proj_scr[r, :, :channels] * scale).astype(BF16)
            k = proj_scr[r, :, channels : 2 * channels].astype(BF16)
            v = proj_scr[r, :, 2 * channels : 3 * channels].astype(BF16)
            gates = jax.nn.sigmoid(proj_scr[r, :, 3 * channels :])
            zero = jnp.zeros((), BF16)
            lane = lax.broadcasted_iota(jnp.int32, (seqs, channels), 1)
            lane_head = lane // depth
            k_block = jnp.concatenate(
                [jnp.where(lane_head // per == g, k, zero) for g in range(halves)], axis=0
            )
            acc = jnp.zeros((seqs, channels), F32)
            for j in range(per):
                qm = jnp.where(lane_head % per == j, q, zero)
                scores = mm_nt(qm, k_block)
                weights = []
                for g in range(halves):
                    sc = jnp.where(masked, MASKED_SCORE, scores[:, g * seqs : (g + 1) * seqs])
                    e = jnp.exp(sc - jnp.max(sc, axis=-1, keepdims=True))
                    weights.append((e * (1.0 / jnp.sum(e, axis=-1, keepdims=True))).astype(BF16))
                v_block = jnp.concatenate(
                    [jnp.where(lane_head == g * per + j, v, zero) for g in range(halves)], axis=0
                )
                acc = acc + mm(jnp.concatenate(weights, axis=1), v_block)
            gated_scr[r] = (acc * gates).astype(BF16)
        second = (
            x.astype(F32) + mm(gated_scr[...].reshape(batch * seqs, channels), wout_ref[...])
        ).astype(BF16)
        second_f = second.astype(F32)
        normed2 = layer_normalize(second_f, gain2_ref[...]).astype(BF16)
        hidden = jnp.maximum(mm(normed2, widen_ref[...]), 0.0).astype(BF16)
        result = (second_f + mm(hidden, shrink_ref[...])).astype(BF16)
        done_scr[pl.ds(i * batch, batch)] = result.reshape(batch, seqs, channels)
        return carry

    lax.fori_loop(0, local_res // batch, body, 0)
    if not turn:
        out_ref[...] = done_scr[...]
    for c in range(slabs):
        for g in range(seqs // SLAB):
            block = done_scr[c * SLAB : (c + 1) * SLAB, g * SLAB : (g + 1) * SLAB]
            turned = mm(swap, block.reshape(SLAB * SLAB, channels))
            out_ref[g * SLAB : (g + 1) * SLAB, c * SLAB : (c + 1) * SLAB] = turned.astype(
                BF16
            ).reshape(SLAB, SLAB, channels)


def whole(count):
    return [pl.BlockSpec(memory_space=pltpu.VMEM)] * count


def body(
    aligned_chain_features,
    pair_representation_state,
    gap_block_flags,
    pair_norm_gain,
    pair_head_weight,
    horizontal_scaling_factor,
    row_input_weight,
    horizontal_final_matrix,
    vertical_scaling_factor,
    column_input_weight,
    vertical_final_matrix,
    feedforward_scaling_factor,
    feedforward_widen_matrix,
    feedforward_shrink_matrix,
):
    groups = lax.axis_size("res")
    here = lax.axis_index("res")
    total_seqs, local_res, channels = aligned_chain_features.shape
    residues = pair_representation_state.shape[1]
    heads = pair_head_weight.shape[1]
    local_seqs = total_seqs // groups
    params = pltpu.CompilerParams(vmem_limit_bytes=VMEM_BYTES)

    arrived = lax.all_to_all(
        aligned_chain_features.reshape(groups, local_seqs, local_res, channels),
        "res", split_axis=0, concat_axis=0, tiled=True,
    )
    bias_local = pl.pallas_call(
        bias_kernel,
        out_shape=jax.ShapeDtypeStruct((heads, local_res, residues), BF16),
        in_specs=whole(3),
        out_specs=pl.BlockSpec(memory_space=pltpu.VMEM),
        scratch_shapes=[pltpu.VMEM((local_res, heads, residues), F32)],
        compiler_params=params,
        name="pair_bias",
    )(pair_representation_state, pair_norm_gain[None, :], pair_head_weight.T)
    bias_all = lax.all_gather(bias_local, "res", axis=0, tiled=False)
    gap_local = lax.dynamic_slice_in_dim(gap_block_flags, here * local_seqs, local_seqs, 0)

    first = pl.pallas_call(
        row_kernel,
        out_shape=jax.ShapeDtypeStruct((groups, local_seqs, local_res, channels), BF16),
        in_specs=[pl.BlockSpec(memory_space=pltpu.SMEM)] + whole(5),
        out_specs=pl.BlockSpec(memory_space=pltpu.VMEM),
        scratch_shapes=[
            pltpu.VMEM((heads, residues, residues), F32),
            pltpu.VMEM((residues, residues * LANES * heads // channels), BF16),
            pltpu.VMEM((residues * LANES * heads // channels, LANES), BF16),
        ],
        compiler_params=params,
        name="row_attention",
    )(
        gap_local, arrived, bias_all, horizontal_scaling_factor[None, :],
        row_input_weight, horizontal_final_matrix,
    )
    back = lax.all_to_all(first, "res", split_axis=0, concat_axis=0, tiled=True)
    back = back.reshape(total_seqs, local_res, channels)
    column_block = (here * local_res) // BLOCK
    col_gap = lax.dynamic_slice_in_dim(gap_block_flags, column_block, 1, 1).reshape(1, total_seqs)
    batch = min(4, local_res)
    turn = local_res % SLAB == 0
    if not turn:
        back = jnp.swapaxes(back, 0, 1)
    done = pl.pallas_call(
        functools.partial(column_kernel, heads, turn),
        out_shape=jax.ShapeDtypeStruct(back.shape, BF16),
        in_specs=whole(8),
        out_specs=pl.BlockSpec(memory_space=pltpu.VMEM),
        scratch_shapes=[
            pltpu.VMEM((local_res, total_seqs, channels), BF16),
            pltpu.VMEM((batch, total_seqs, 4 * channels), F32),
            pltpu.VMEM((batch, total_seqs, channels), BF16),
            pltpu.VMEM((total_seqs, 2 * total_seqs), BF16),
            pltpu.VMEM((local_res, total_seqs, channels), BF16),
        ],
        compiler_params=params,
        name="column_transition",
    )(
        col_gap, back, vertical_scaling_factor[None, :], column_input_weight,
        vertical_final_matrix, feedforward_scaling_factor[None, :],
        feedforward_widen_matrix, feedforward_shrink_matrix,
    )
    return done if turn else jnp.swapaxes(done, 0, 1)


def solution(mesh):
    placed = (
        P("dp", "res", None),
        P(("dp", "res"), None, None),
        P("dp", None),
    ) + (P(),) * 11
    return jax.shard_map(
        body, mesh=mesh, in_specs=placed, out_specs=P("dp", "res", None), check_vma=False
    )
```

time: 325 us -> 203 us (0.62)
  matrix products: 134 us -> 0 us
  Pallas kernels: 0 us -> 69.4 us
  other arithmetic: 37.7 us -> 0 us
  local copies, waits for them, and re-layouts: 25.5 us -> 3.79 us
  waiting for transfers between devices: 100 us -> 105 us
    dot_general x39 -> x0, matrix products: 98.2 us -> none  [the longest x16 40.3 us: attend_dense(): jnp.einsum('hqk,khd->qhd', weights_bf, values_bf, preferred_element_type=...]
    pallas_call x0 -> x3, Pallas kernels: none -> 69.4 us  [the longest x1 34.5 us: body(): pl.pallas_call(functools.partial(column_kernel, heads, turn), out_shape=j...]
    sub x16 -> x0, matrix products: 36 us -> none  [attend_dense(): weights_bf = jax.nn.softmax(scores, axis=-1).astype(jnp.bfloat16)]
    sub x1 -> x0, other arithmetic: 18.1 us -> none  [body(): col_weights = jax.nn.softmax(col_scores, axis=-1).astype(jnp.bfloat16)]
    reduce_sum x8 -> x0, other arithmetic: 11.2 us -> none  [the longest x4 7.56 us: layer_normalize(): spread = jnp.mean(centred * centred, axis=-1, keepdims=True)]
    convert_element_type x3 -> x0, local copies, waits for them, and re-layouts: 9.35 us -> none  [the longest x1 4.08 us: body(): return (alignment_second.astype(jnp.float32) + jnp.dot(tr_hidden, feedfor...]
    while x2 -> x0, local copies, waits for them, and re-layouts: 4.94 us -> none  [body(): lax.map(per_sequence, (queries, keys_all, values_all, gates_all, sequence...]
    unnamed x31, local copies, waits for them, and re-layouts: 8.35 us -> 3.71 us
  transfers between devices with their start and end apart: 3 -> 3, of which waited for: 2 -> 2; matrix products, arithmetic and copies ran while one was open for 5% -> 0% of each run, Pallas kernels for 0% -> 2%
where the time goes in v1:
time: 203 us
  waiting for transfers between devices  105 us (52%)
  Pallas kernels  69.4 us (34%)
  between operations  13.5 us (7%)
  starting transfers between devices  11.4 us (6%)
  local copies, waits for them, and re-layouts  3.79 us (2%)
    all_gather x1, waiting for transfers between devices, body(): bias_all = lax.all_gather(bias_local, 'res', axis=0, tiled=False)  57.2 us
    all_to_all x1, waiting for transfers between devices, body(): back = lax.all_to_all(first, 'res', split_axis=0, concat_axis=0, tiled=True)  47.4 us
    pallas_call x1, Pallas kernels, body(): pl.pallas_call(functools.partial(column_kernel, heads, turn), out_shape=j...  34.5 us
    pallas_call x1, Pallas kernels, body(): pl.pallas_call(row_kernel, out_shape=jax.ShapeDtypeStruct((groups, local_...  30.2 us
    all_to_all x1, starting transfers between devices, body(): lax.all_to_all(aligned_chain_features.reshape(groups, local_seqs, local_r...  7.42 us
    pallas_call x1, Pallas kernels, body(): pl.pallas_call(bias_kernel, out_shape=jax.ShapeDtypeStruct((heads, local_...  4.64 us
  transfers between devices with their start and end apart: 3, of which 2 were waited for; matrix products, arithmetic and copies ran while one was open for 0% of the time, Pallas kernels for 2%

profile of v1, /device:TPU:0, one launch (start us, length us, event | category | flops | bytes accessed | tf_op | source)
XLA Modules:
  0.0 202.7 jit_solution(13602278264966752124)
XLA Ops:
  6.5 0.0 copy-start
  6.5 7.4 %all-to-all-start = ((bf16[8,16,32,256]{3,2,1,0:T(8,128)(2,1)}), bf16[8,16,32,256]{3,2,1,0:T(8,128)(2,1)}, u32[]{:S(2)}, u32[]{:S(2)}) async-start(bf16[8,16,32,256]{3,2,1,0:T(8,128)(2,1)} %bitcast.17), calls=%async_computation | async-start | bytes 4194304 | tf_op jit(solution)/shard_map/all_to_all | solution.py:216
  14.0 0.0 copy-start.8
  14.0 0.0 copy-start.11
  14.0 0.0 all-gather.3.cloned.1.call-start
  14.0 0.0 copy-done.2
  14.1 0.0 copy-done.10
  14.1 0.0 copy-done.14
  14.1 4.6 %pair_bias.1 = bf16[8,32,256]{2,1,0:T(8,128)(2,1)} custom-call(bf16[32,256,128]{2,1,0:T(8,128)(2,1)S(1)} %copy-done.2, f32[1,128]{1,0:T(1,128)S(1)} %bitcast.16, bf16[8,128]{1,0:T(8,128)(2,1)S(1)} %bitcast.12), custom_call_target="tpu_custom_call" | custom-call | tf_op jit(solution)/shard_map/pair_bias/pallas_call | solution.py:220
  18.7 0.0 all-gather.3.cloned.1.call-update
  18.7 0.0 copy-done
  18.8 0.1 constant_dynamic-slice_fusion
  18.8 0.1 copy.17.gap_ref
  18.9 57.2 %all-gather.3.cloned.1.call-done = bf16[64,32,256]{2,1,0:T(8,128)(2,1)} async-done(((bf16[8,32,256]{2,1,0:T(8,128)(2,1)}), bf16[64,32,256]{2,1,0:T(8,128)(2,1)}) %all-gather.3.cloned.1.call-update) | async-done | bytes 1048592 | tf_op jit(solution)/shard_map/all_gather | solution.py:229
  76.1 0.0 all-to-all-done.x_ref
  76.1 0.0 copy-done.4
  76.1 0.0 copy-done.8
  76.1 0.0 copy-done.11
  76.1 0.0 copy-start.3
  76.1 1.2 copy-done.3
  77.3 30.2 %row_attention.1 = bf16[8,16,32,256]{3,2,1,0:T(8,128)(2,1)S(1)} custom-call(s32[16,2]{1,0:T(8,128)S(1)} %copy.17.gap_ref, bf16[8,16,32,256]{3,2,1,0:T(8,128)(2,1)} %all-to-all-done.x_ref, bf16[8,8,32,256]{3,2,1,0:T(8,128)(2,1)S(1)} %bitcast.11, f32[1,256]{1,0:T(1,128)S(1)} %bitcast.13, bf16[256,1024]{1,0:T(8,128)(2,1)S(1)} %copy-done.4, ...), custom_call_target="tpu_custom_call" | custom-call | tf_op jit(solution)/shard_map/row_attention/pallas_call | solution.py:232
  107.5 0.0 copy-start.1
  107.5 1.3 copy-done.1
  108.8 0.0 copy-start.13
  108.9 3.9 %all-to-all-start.1 = ((bf16[8,16,32,256]{3,2,1,0:T(8,128)(2,1)}), bf16[8,16,32,256]{3,2,1,0:T(8,128)(2,1)S(1)}, u32[]{:S(2)}, u32[]{:S(2)}) async-start(bf16[8,16,32,256]{3,2,1,0:T(8,128)(2,1)} %copy-done.1), calls=%async_computation.1 | async-start | bytes 4194304 | tf_op jit(solution)/shard_map/all_to_all | solution.py:248
  112.8 47.4 %all-to-all-done.1 = bf16[8,16,32,256]{3,2,1,0:T(8,128)(2,1)S(1)} async-done(((bf16[8,16,32,256]{3,2,1,0:T(8,128)(2,1)}), bf16[8,16,32,256]{3,2,1,0:T(8,128)(2,1)S(1)}, u32[]{:S(2)}, u32[]{:S(2)}) %all-to-all-start.1) | async-done | bytes 2097184 | tf_op jit(solution)/shard_map/all_to_all | solution.py:248
  160.2 0.0 copy-done.5
  160.2 0.0 copy-done.6
  160.2 0.0 copy-done.9
  160.3 0.0 copy-start.7
  160.3 1.0 copy-done.7
  161.3 34.5 %column_transition.1 = bf16[128,32,256]{2,1,0:T(8,128)(2,1)} custom-call(s32[1,128]{1,0:T(1,128)S(1)} %dynamic-slice_bitcast_fusion.gap_ref, bf16[128,32,256]{2,1,0:T(8,128)(2,1)S(1)} %bitcast.10, f32[1,256]{1,0:T(1,128)S(1)} %bitcast.14, bf16[256,1024]{1,0:T(8,128)(2,1)S(1)} %copy-done.5, bf16[256,256]{1,0:T(8,128)(2,1)S(1)} %copy-done.9, ...), custom_call_target="tpu_custom_call" | custom-call | tf_op jit(solution)/shard_map/column_transition/pallas_call | solution.py:256
  (11 shorter events, 0.0 us)
Async XLA Ops:
  6.5 12.2 %copy-start = (s32[128,2]{0,1:T(2,128)S(1)}, s32[128,2]{0,1:T(2,128)}, u32[]{:S(2)}) copy-start(s32[128,2]{0,1:T(2,128)} %param.16) | copy-start | bytes 3076
  6.5 7.5 %copy-start.2 = (bf16[32,256,128]{2,1,0:T(8,128)(2,1)S(1)}, bf16[32,256,128]{2,1,0:T(8,128)(2,1)}, u32[]{:S(2)}) copy-start(bf16[32,256,128]{2,1,0:T(8,128)(2,1)} %pair_ref.1) | copy-start | bytes 6291460
  6.5 7.5 %copy-start.10 = (bf16[128,8]{0,1:T(8,128)(2,1)S(1)}, bf16[128,8]{0,1:T(8,128)(2,1)}, u32[]{:S(2)}) copy-start(bf16[128,8]{0,1:T(8,128)(2,1)} %param.18) | copy-start | bytes 6148
  6.5 7.5 %copy-start.14 = (f32[128]{0:T(128)S(1)}, f32[128]{0:T(128)}, u32[]{:S(2)}) copy-start(f32[128]{0:T(128)} %param.17) | copy-start | bytes 1540
  6.5 69.5 %all-to-all-start = ((bf16[8,16,32,256]{3,2,1,0:T(8,128)(2,1)}), bf16[8,16,32,256]{3,2,1,0:T(8,128)(2,1)}, u32[]{:S(2)}, u32[]{:S(2)}) async-start(bf16[8,16,32,256]{3,2,1,0:T(8,128)(2,1)} %bitcast.17), calls=%async_computation | async-start | bytes 4194304 | tf_op jit(solution)/shard_map/all_to_all | solution.py:216
  14.0 62.1 %copy-start.4 = (bf16[256,1024]{1,0:T(8,128)(2,1)S(1)}, bf16[256,1024]{1,0:T(8,128)(2,1)}, u32[]{:S(2)}) copy-start(bf16[256,1024]{1,0:T(8,128)(2,1)} %win_ref.2) | copy-start | bytes 1572868
  14.0 62.1 %copy-start.8 = (bf16[256,256]{1,0:T(8,128)(2,1)S(1)}, bf16[256,256]{1,0:T(8,128)(2,1)}, u32[]{:S(2)}) copy-start(bf16[256,256]{1,0:T(8,128)(2,1)} %wout_ref.2) | copy-start | bytes 393220
  14.0 62.1 %copy-start.11 = (f32[256]{0:T(256)S(1)}, f32[256]{0:T(256)}, u32[]{:S(2)}) copy-start(f32[256]{0:T(256)} %param.19) | copy-start | bytes 3076
  14.0 62.1 %all-gather.3.cloned.1.call-start = ((), (), s32[]{:S(2)}) async-start(), calls=%async_computation.2 | async-start | bytes 1179648 | tf_op jit(solution)/shard_map/all_gather | solution.py:229
  76.1 1.2 copy-start.3
  107.5 1.3 copy-start.1
  108.8 51.4 %copy-start.5 = (bf16[256,1024]{1,0:T(8,128)(2,1)S(1)}, bf16[256,1024]{1,0:T(8,128)(2,1)}, u32[]{:S(2)}) copy-start(bf16[256,1024]{1,0:T(8,128)(2,1)} %win_ref.3) | copy-start | bytes 1572868
  108.8 51.4 %copy-start.6 = (bf16[256,1024]{1,0:T(8,128)(2,1)S(1)}, bf16[256,1024]{1,0:T(8,128)(2,1)}, u32[]{:S(2)}) copy-start(bf16[256,1024]{1,0:T(8,128)(2,1)} %widen_ref.1) | copy-start | bytes 1572868
  108.8 51.4 %copy-start.9 = (bf16[256,256]{1,0:T(8,128)(2,1)S(1)}, bf16[256,256]{1,0:T(8,128)(2,1)}, u32[]{:S(2)}) copy-start(bf16[256,256]{1,0:T(8,128)(2,1)} %wout_ref.3) | copy-start | bytes 393220
  108.8 51.4 %copy-start.12 = (f32[256]{0:T(256)S(1)}, f32[256]{0:T(256)}, u32[]{:S(2)}) copy-start(f32[256]{0:T(256)} %param.22) | copy-start | bytes 3076
  108.8 51.4 %copy-start.13 = (f32[256]{0:T(256)S(1)}, f32[256]{0:T(256)}, u32[]{:S(2)}) copy-start(f32[256]{0:T(256)} %param.25) | copy-start | bytes 3076
  108.9 51.4 %all-to-all-start.1 = ((bf16[8,16,32,256]{3,2,1,0:T(8,128)(2,1)}), bf16[8,16,32,256]{3,2,1,0:T(8,128)(2,1)S(1)}, u32[]{:S(2)}, u32[]{:S(2)}) async-start(bf16[8,16,32,256]{3,2,1,0:T(8,128)(2,1)} %copy-done.1), calls=%async_computation.1 | async-start | bytes 4194304 | tf_op jit(solution)/shard_map/all_to_all | solution.py:248
  160.3 1.0 copy-start.7
Sparse Core Ops, SparseCore 0:
  18.9 57.1 all-gather.2
